TPU v7x, 32 devices: a whole 2x2x4 slice. The times are simulated.
32 devices in a mesh: groups: 2 (over y), dp: 8 (over z, x), tensor: 2 (over core).
Axes of the slice: x: 2, y: 2, z: 4, core: 2. Of those that a mesh axis runs over, the one named last changes fastest.
Arguments:
- inputs_t: bfloat16 [8192, 2048], P('tensor', ('groups', 'dp')), parts along dimension 1, may hold values from -6 to 6
- cotangent_t: bfloat16 [8192, 2048], P('tensor', ('groups', 'dp')), parts along dimension 1, may hold values from -6 to 6
- adapter_down: bfloat16 [128, 16, 8192], P(('groups', 'dp'), None, 'tensor'), parts along dimension 0, may hold values from -0.0625 to 0.0625
- adapter_up: bfloat16 [128, 16, 8192], P(('groups', 'dp'), None, 'tensor'), parts along dimension 0, may hold values from -1.5 to 1.5
- block_tenant: int32 [16], P(('groups', 'dp')), parts along dimension 0, may hold values from 0 to 63
- block_rows: int32 [16], P(('groups', 'dp')), parts along dimension 0, may hold values from 0 to 128, as said below
- owner_slot: int32 [128], P('groups'), parts along dimension 0, may hold values from 0 to 63, as said below
Outputs:
- delta_t: bfloat16 [8192, 2048], P('tensor', ('groups', 'dp')), parts along dimension 1
- grad_input_t: bfloat16 [8192, 2048], P('tensor', ('groups', 'dp')), parts along dimension 1
- grad_down: float32 [128, 16, 8192], P(('groups', 'dp'), None, 'tensor'), parts along dimension 0
- grad_up: float32 [128, 16, 8192], P(('groups', 'dp'), None, 'tensor'), parts along dimension 0
There are 2 independent parts, one for each index of `groups`. A program takes and returns all parts, laid end to end along the dimension named above; each array names one. Nothing has to cross between parts.
Inputs may be any that keep to these rules, and one draw needn't show every extreme that they name: `block_rows`: each block's count of live token slots; live slots come first in a block. `owner_slot`: distinct slots, one for each tenant.
All inputs are finite; a program needn't handle non-finite values.
Results may differ from a plain program's by a relative error of at most 0.0051.
Values may be sent and summed in bfloat16 or wider, within the bound.
A program may use at most 64 MiB of HBM per device.

v0:
```python
import jax
import jax.numpy as jnp
from jax import lax
from jax.sharding import PartitionSpec as P

adapter_scale_factor = 2.0
grad_scale = 0.125


def shards(inputs_t, cotangent_t, adapter_down, adapter_up, block_tenant, block_rows, owner_slot):
    local_width, local_rows = inputs_t.shape
    slots_dev = block_rows.shape[0]
    block_size = local_rows // slots_dev
    devices = lax.axis_size("dp")
    tenants = owner_slot.shape[0]
    own_dev = adapter_down.shape[0]
    total_slots = own_dev * devices
    positions = jnp.arange(local_rows, dtype=jnp.int32)
    valid = positions % block_size < jnp.repeat(
        block_rows, block_size, total_repeat_length=local_rows
    )
    keeping = valid.astype(jnp.bfloat16)
    masked_in = inputs_t * keeping[None, :]
    masked_grad = cotangent_t * keeping[None, :]
    matches = block_tenant[:, None] == jnp.arange(tenants, dtype=jnp.int32)[None, :]
    my_slot = jnp.sum(jnp.where(matches, owner_slot[None, :], 0), axis=1)
    every_slot = lax.all_gather(my_slot, "dp", axis=0, tiled=True)
    picker = (every_slot[:, None] == jnp.arange(total_slots, dtype=jnp.int32)[None, :]).astype(
        jnp.bfloat16
    )
    down_piece, up_piece = (
        lax.all_to_all(adapter_down, "dp", split_axis=2, concat_axis=0, tiled=True),
        lax.all_to_all(adapter_up, "dp", split_axis=2, concat_axis=0, tiled=True),
    )
    chosen_down = jnp.einsum(
        "bs,srf->brf", picker, down_piece, preferred_element_type=jnp.float32
    ).astype(jnp.bfloat16)
    chosen_up = jnp.einsum(
        "bs,srf->brf", picker, up_piece, preferred_element_type=jnp.float32
    ).astype(jnp.bfloat16)
    picker_float = picker.astype(jnp.float32)
    mine_down, mine_up = (
        lax.all_to_all(chosen_down, "dp", split_axis=0, concat_axis=2, tiled=True),
        lax.all_to_all(chosen_up, "dp", split_axis=0, concat_axis=2, tiled=True),
    )
    token_blocks = masked_in.reshape(local_width, slots_dev, block_size)
    grad_blocks = masked_grad.reshape(local_width, slots_dev, block_size)
    low_part = jnp.einsum(
        "brd,dbc->rbc", mine_down, token_blocks, preferred_element_type=jnp.float32
    )
    back_part = jnp.einsum("brd,dbc->rbc", mine_up, grad_blocks, preferred_element_type=jnp.float32)
    low_sum, back_sum = lax.psum((low_part, back_part), "tensor")
    rounded_low_rank = low_sum.astype(jnp.bfloat16)
    backward_rounded = back_sum.astype(jnp.bfloat16)
    delta_t = (
        (
            adapter_scale_factor
            * jnp.einsum(
                "brd,rbc->dbc", mine_up, rounded_low_rank, preferred_element_type=jnp.float32
            )
        )
        .astype(jnp.bfloat16)
        .reshape(local_width, local_rows)
    )
    grad_input_t = (
        (
            adapter_scale_factor
            * jnp.einsum(
                "brd,rbc->dbc", mine_down, backward_rounded, preferred_element_type=jnp.float32
            )
        )
        .astype(jnp.bfloat16)
        .reshape(local_width, local_rows)
    )
    block_down = jnp.einsum(
        "rbc,dbc->brd", backward_rounded, token_blocks, preferred_element_type=jnp.float32
    )
    block_up = jnp.einsum(
        "rbc,dbc->brd", rounded_low_rank, grad_blocks, preferred_element_type=jnp.float32
    )
    spread_down, spread_up = (
        lax.all_to_all(block_down, "dp", split_axis=2, concat_axis=0, tiled=True),
        lax.all_to_all(block_up, "dp", split_axis=2, concat_axis=0, tiled=True),
    )
    sum_down = jnp.einsum("bs,brf->srf", picker_float, spread_down, precision=lax.Precision.HIGHEST)
    sum_up = jnp.einsum("bs,brf->srf", picker_float, spread_up, precision=lax.Precision.HIGHEST)
    grad_down, grad_up = (
        lax.all_to_all(grad_scale * sum_down, "dp", split_axis=0, concat_axis=2, tiled=True),
        lax.all_to_all(grad_scale * sum_up, "dp", split_axis=0, concat_axis=2, tiled=True),
    )
    return (delta_t, grad_input_t, grad_down, grad_up)


def solution(mesh):
    return jax.shard_map(
        shards,
        mesh=mesh,
        in_specs=(
            P("tensor", ("groups", "dp")),
            P("tensor", ("groups", "dp")),
            P(("groups", "dp"), None, "tensor"),
            P(("groups", "dp"), None, "tensor"),
            P(("groups", "dp")),
            P(("groups", "dp")),
            P("groups"),
        ),
        out_specs=(
            P("tensor", ("groups", "dp")),
            P("tensor", ("groups", "dp")),
            P(("groups", "dp"), None, "tensor"),
            P(("groups", "dp"), None, "tensor"),
        ),
        check_vma=False,
    )
```

profile of v0, /device:TPU:0, one launch (start us, length us, event | category | flops | bytes accessed | tf_op | source)
XLA Modules:
  0.0 313.3 jit_solution(13265155162579666002)
XLA Ops:
  0.6 8.2 %copy.37 = bf16[8,16,4096]{1,0,2:T(8,128)(2,1)} copy(bf16[8,16,4096]{2,1,0:T(8,128)(2,1)} %param.14) | data formatting | bytes 2097152 | tf_op args[3]
  8.9 11.2 %reshape.147 = bf16[8,2,32768]{2,1,0:T(2,128)(2,1)} reshape(bf16[4096,8,16]{2,1,0:T(8,128)(2,1)} %bitcast.110) | data formatting | bytes 2097152
  20.1 7.4 %all-to-all-start.2 = ((bf16[8,2,32768]{2,1,0:T(2,128)(2,1)}), bf16[8,2,32768]{2,1,0:T(2,128)(2,1)S(1)}, u32[]{:S(2)}, u32[]{:S(2)}) async-start(bf16[8,2,32768]{2,1,0:T(2,128)(2,1)} %reshape.147), calls=%async_computation.2 | async-start | bytes 2097152 | tf_op jit(solution)/shard_map/all_to_all | solution.py:33
  27.5 7.3 %copy.33 = bf16[8,16,4096]{1,0,2:T(8,128)(2,1)} copy(bf16[8,16,4096]{2,1,0:T(8,128)(2,1)S(1)} %copy-done.3) | data formatting | bytes 2097152 | tf_op args[2]
  34.8 11.2 %reshape.149 = bf16[8,2,32768]{2,1,0:T(2,128)(2,1)} reshape(bf16[4096,8,16]{2,1,0:T(8,128)(2,1)} %bitcast.111) | data formatting | bytes 2097152
  46.1 7.2 %all-to-all-done.2 = bf16[8,2,32768]{2,1,0:T(2,128)(2,1)S(1)} async-done(((bf16[8,2,32768]{2,1,0:T(2,128)(2,1)}), bf16[8,2,32768]{2,1,0:T(2,128)(2,1)S(1)}, u32[]{:S(2)}, u32[]{:S(2)}) %all-to-all-start.2) | async-done | bytes 1048608 | tf_op jit(solution)/shard_map/all_to_all | solution.py:33
  60.1 22.8 %all-reduce = s32[8]{0:T(128)S(1)} all-reduce(s32[8]{0:T(128)S(1)} %dynamic-update-slice.6), channel_id=1, replica_groups=mesh['groups'=2,'dp'=8,'tensor'=2] {'dp'}, use_global_device_ids=true, to_apply=%add | all-reduce | flops 8 | bytes 64
  83.0 7.5 %reshape.148 = bf16[4096,8,16]{2,1,0:T(8,128)(2,1)} reshape(bf16[8,2,32768]{2,1,0:T(2,128)(2,1)S(1)} %all-to-all-done.2) | data formatting | bytes 2097152
  90.5 9.1 %copy.38 = bf16[8,16,8,512]{3,0,2,1:T(8,128)(2,1)S(1)} copy(bf16[8,16,8,512]{1,0,3,2:T(8,128)(2,1)} %bitcast.108) | data formatting | bytes 2097152 | tf_op jit(solution)/shard_map/all_to_all | solution.py:33
  100.6 3.6 %all-to-all-start.3 = ((bf16[8,16,512]{2,1,0:T(8,128)(2,1)}), bf16[8,16,512]{2,1,0:T(8,128)(2,1)S(1)}, u32[]{:S(2)}, u32[]{:S(2)}) async-start(bf16[8,16,512]{2,1,0:T(8,128)(2,1)} %copy.39), calls=%async_computation.3 | async-start | bytes 262144 | tf_op jit(solution)/shard_map/all_to_all | solution.py:44
  104.3 7.5 %reshape.150 = bf16[4096,8,16]{2,1,0:T(8,128)(2,1)} reshape(bf16[8,2,32768]{2,1,0:T(2,128)(2,1)S(1)} %all-to-all-done) | data formatting | bytes 2097152
  111.8 9.1 %copy.34 = bf16[8,16,8,512]{3,0,2,1:T(8,128)(2,1)S(1)} copy(bf16[8,16,8,512]{1,0,3,2:T(8,128)(2,1)} %bitcast.109) | data formatting | bytes 2097152 | tf_op jit(solution)/shard_map/all_to_all | solution.py:32
  122.0 6.0 %all-to-all-start.1 = ((bf16[8,16,512]{2,1,0:T(8,128)(2,1)}), bf16[8,16,512]{2,1,0:T(8,128)(2,1)S(1)}, u32[]{:S(2)}, u32[]{:S(2)}) async-start(bf16[8,16,512]{2,1,0:T(8,128)(2,1)} %copy.35), calls=%async_computation.1 | async-start | bytes 262144 | tf_op jit(solution)/shard_map/all_to_all | solution.py:43
  128.6 6.7 %all-to-all-done.1 = bf16[8,16,512]{2,1,0:T(8,128)(2,1)S(1)} async-done(((bf16[8,16,512]{2,1,0:T(8,128)(2,1)}), bf16[8,16,512]{2,1,0:T(8,128)(2,1)S(1)}, u32[]{:S(2)}, u32[]{:S(2)}) %all-to-all-start.1) | async-done | bytes 131104 | tf_op jit(solution)/shard_map/all_to_all | solution.py:43
  140.0 19.3 %reduce.6 = f32[4096,16]{1,0:T(8,128)} reduce(f32[4096,1,16]{2,1,0:T(1,128)S(1)} %bitcast.115, f32[]{:T(128)} %broadcast.104), dimensions={1}, to_apply=%bitcast.98.reduce_sub_computation | reduce | bytes 524292
  162.5 4.1 %all-to-all-start.4 = ((f32[8,1,8192]{2,1,0:T(1,128)}), f32[8,1,8192]{2,1,0:T(1,128)}, u32[]{:S(2)}, u32[]{:S(2)}) async-start(f32[8,1,8192]{2,1,0:T(1,128)} %reshape.151), calls=%async_computation.4 | async-start | bytes 524288 | tf_op jit(solution)/shard_map/all_to_all | solution.py:82
  166.9 19.3 %reduce.8 = f32[4096,16]{1,0:T(8,128)} reduce(f32[4096,1,16]{2,1,0:T(1,128)S(1)} %bitcast.116, f32[]{:T(128)} %broadcast.104), dimensions={1}, to_apply=%bitcast.100.reduce_sub_computation | reduce | bytes 524292
  189.3 5.9 %all-to-all-start.6 = ((f32[8,1,8192]{2,1,0:T(1,128)}), f32[8,1,8192]{2,1,0:T(1,128)S(1)}, u32[]{:S(2)}, u32[]{:S(2)}) async-start(f32[8,1,8192]{2,1,0:T(1,128)} %reshape.153), calls=%async_computation.6 | async-start | bytes 524288 | tf_op jit(solution)/shard_map/all_to_all | solution.py:83
  197.4 3.9 %reshape.152 = f32[4096,1,16]{2,1,0:T(1,128)S(1)} reshape(f32[8,8192]{1,0:T(8,128)S(1)} %reduce.7) | data formatting | bytes 524288
  205.6 6.0 %all-to-all-start.5 = ((f32[64,16,512]{2,1,0:T(8,128)}), f32[64,16,512]{2,1,0:T(8,128)}, u32[]{:S(2)}, u32[]{:S(2)}) async-start(f32[64,16,512]{2,1,0:T(8,128)} %copy.43), calls=%async_computation.5 | async-start | bytes 4194304 | tf_op jit(solution)/shard_map/all_to_all | solution.py:88
  212.9 3.9 %reshape.154 = f32[4096,1,16]{2,1,0:T(1,128)S(1)} reshape(f32[8,8192]{1,0:T(8,128)S(1)} %reduce.9) | data formatting | bytes 524288
  221.1 38.5 %all-to-all-done.5 = f32[64,16,512]{2,1,0:T(8,128)} async-done(((f32[64,16,512]{2,1,0:T(8,128)}), f32[64,16,512]{2,1,0:T(8,128)}, u32[]{:S(2)}, u32[]{:S(2)}) %all-to-all-start.5) | async-done | bytes 2097184 | tf_op jit(solution)/shard_map/all_to_all | solution.py:88
  259.6 3.6 %all-to-all-start.7 = ((f32[64,16,512]{2,1,0:T(8,128)}), f32[64,16,512]{2,1,0:T(8,128)S(1)}, u32[]{:S(2)}, u32[]{:S(2)}) async-start(f32[64,16,512]{2,1,0:T(8,128)} %copy.47), calls=%async_computation.7 | async-start | bytes 4194304 | tf_op jit(solution)/shard_map/all_to_all | solution.py:89
  270.0 41.7 %all-to-all-done.7 = f32[64,16,512]{2,1,0:T(8,128)S(1)} async-done(((f32[64,16,512]{2,1,0:T(8,128)}), f32[64,16,512]{2,1,0:T(8,128)S(1)}, u32[]{:S(2)}, u32[]{:S(2)}) %all-to-all-start.7) | async-done | bytes 2097184 | tf_op jit(solution)/shard_map/all_to_all | solution.py:89
  (50 shorter events, 39.7 us)
Async XLA Ops:
  20.1 7.4 %copy-start.3 = (bf16[8,16,4096]{2,1,0:T(8,128)(2,1)S(1)}, bf16[8,16,4096]{2,1,0:T(8,128)(2,1)}, u32[]{:S(2)}) copy-start(bf16[8,16,4096]{2,1,0:T(8,128)(2,1)} %param.13) | copy-start | bytes 3145732
  20.1 33.2 %all-to-all-start.2 = ((bf16[8,2,32768]{2,1,0:T(2,128)(2,1)}), bf16[8,2,32768]{2,1,0:T(2,128)(2,1)S(1)}, u32[]{:S(2)}, u32[]{:S(2)}) async-start(bf16[8,2,32768]{2,1,0:T(2,128)(2,1)} %reshape.147), calls=%async_computation.2 | async-start | bytes 2097152 | tf_op jit(solution)/shard_map/all_to_all | solution.py:33
  46.1 11.4 %copy-start.5 = (u32[32]{0:T(128)S(1)}, u32[32]{0:T(128)}, u32[]{:S(2)}) copy-start(u32[32]{0:T(128)} %constant.115) | copy-start | bytes 388
  46.1 12.0 %copy-start.4 = (s32[64]{0:T(128)S(1)}, s32[64]{0:T(128)}, u32[]{:S(2)}) copy-start(s32[64]{0:T(128)} %param.17) | copy-start | bytes 772
  53.3 47.4 %all-to-all-start = ((bf16[8,2,32768]{2,1,0:T(2,128)(2,1)}), bf16[8,2,32768]{2,1,0:T(2,128)(2,1)S(1)}, u32[]{:S(2)}, u32[]{:S(2)}) async-start(bf16[8,2,32768]{2,1,0:T(2,128)(2,1)} %reshape.149), calls=%async_computation | async-start | bytes 2097152 | tf_op jit(solution)/shard_map/all_to_all | solution.py:32
  100.6 21.3 %all-to-all-start.3 = ((bf16[8,16,512]{2,1,0:T(8,128)(2,1)}), bf16[8,16,512]{2,1,0:T(8,128)(2,1)S(1)}, u32[]{:S(2)}, u32[]{:S(2)}) async-start(bf16[8,16,512]{2,1,0:T(8,128)(2,1)} %copy.39), calls=%async_computation.3 | async-start | bytes 262144 | tf_op jit(solution)/shard_map/all_to_all | solution.py:44
  120.9 14.4 %copy-start = (bf16[4096,128]{1,0:T(8,128)(2,1)S(1)}, bf16[4096,128]{1,0:T(8,128)(2,1)}, u32[]{:S(2)}) copy-start(bf16[4096,128]{1,0:T(8,128)(2,1)} %param.11) | copy-start | bytes 3145732
  120.9 14.6 %copy-start.1 = (bf16[4096,128]{1,0:T(8,128)(2,1)S(1)}, bf16[4096,128]{1,0:T(8,128)(2,1)}, u32[]{:S(2)}) copy-start(bf16[4096,128]{1,0:T(8,128)(2,1)} %param.12) | copy-start | bytes 3145732
  122.0 13.3 %all-to-all-start.1 = ((bf16[8,16,512]{2,1,0:T(8,128)(2,1)}), bf16[8,16,512]{2,1,0:T(8,128)(2,1)S(1)}, u32[]{:S(2)}, u32[]{:S(2)}) async-start(bf16[8,16,512]{2,1,0:T(8,128)(2,1)} %copy.35), calls=%async_computation.1 | async-start | bytes 262144 | tf_op jit(solution)/shard_map/all_to_all | solution.py:43
  159.4 7.1 %copy-start.2 = (bf16[4096,128]{1,0:T(8,128)(2,1)S(1)}, bf16[4096,128]{1,0:T(8,128)(2,1)}, u32[]{:S(2)}) copy-start(bf16[4096,128]{1,0:T(8,128)(2,1)} %param.12) | copy-start | bytes 3145732
  162.5 26.8 %all-to-all-start.4 = ((f32[8,1,8192]{2,1,0:T(1,128)}), f32[8,1,8192]{2,1,0:T(1,128)}, u32[]{:S(2)}, u32[]{:S(2)}) async-start(f32[8,1,8192]{2,1,0:T(1,128)} %reshape.151), calls=%async_computation.4 | async-start | bytes 524288 | tf_op jit(solution)/shard_map/all_to_all | solution.py:82
  189.3 16.3 %all-to-all-start.6 = ((f32[8,1,8192]{2,1,0:T(1,128)}), f32[8,1,8192]{2,1,0:T(1,128)S(1)}, u32[]{:S(2)}, u32[]{:S(2)}) async-start(f32[8,1,8192]{2,1,0:T(1,128)} %reshape.153), calls=%async_computation.6 | async-start | bytes 524288 | tf_op jit(solution)/shard_map/all_to_all | solution.py:83
  205.6 54.0 %all-to-all-start.5 = ((f32[64,16,512]{2,1,0:T(8,128)}), f32[64,16,512]{2,1,0:T(8,128)}, u32[]{:S(2)}, u32[]{:S(2)}) async-start(f32[64,16,512]{2,1,0:T(8,128)} %copy.43), calls=%async_computation.5 | async-start | bytes 4194304 | tf_op jit(solution)/shard_map/all_to_all | solution.py:88
  259.6 52.1 %all-to-all-start.7 = ((f32[64,16,512]{2,1,0:T(8,128)}), f32[64,16,512]{2,1,0:T(8,128)S(1)}, u32[]{:S(2)}, u32[]{:S(2)}) async-start(f32[64,16,512]{2,1,0:T(8,128)} %copy.47), calls=%async_computation.7 | async-start | bytes 4194304 | tf_op jit(solution)/shard_map/all_to_all | solution.py:89
where the time goes:
time: 315 us; the launch traced here: 313 us
  local copies, waits for them, and re-layouts  103 us (33%)
  waiting for transfers between devices  94.1 us (30%)
  other arithmetic  42.8 us (14%)
  starting transfers between devices  40.2 us (13%)
  blocking collectives  26.2 us (8%)
  matrix products  4.98 us (2%)
    unnamed x30, local copies, waits for them, and re-layouts  72.2 us
    all_to_all x1, waiting for transfers between devices, shards(): lax.all_to_all(grad_scale * sum_up, 'dp', split_axis=0, concat_axis=2, ti...  41.7 us
    unnamed x2, other arithmetic  38.7 us
    all_to_all x1, waiting for transfers between devices, shards(): lax.all_to_all(grad_scale * sum_down, 'dp', split_axis=0, concat_axis=2,...  38.5 us
    unnamed x1, blocking collectives  22.8 us
    all_to_all x1, local copies, waits for them, and re-layouts, shards(): lax.all_to_all(adapter_up, 'dp', split_axis=2, concat_axis=0, tiled=True)  9.13 us
    all_to_all x1, local copies, waits for them, and re-layouts, shards(): lax.all_to_all(adapter_down, 'dp', split_axis=2, concat_axis=0, tiled=True)  9.13 us
    all_to_all x1, starting transfers between devices, shards(): lax.all_to_all(adapter_up, 'dp', split_axis=2, concat_axis=0, tiled=True)  7.38 us
  transfers between devices with their start and end apart: 8, of which 4 were waited for; matrix products, arithmetic and copies ran while one was open for 34% of the time, Pallas kernels for 0%

commit v1 on v0

v1 whole, which is shorter than its diff:
```python
import functools
import jax
import jax.numpy as jnp
from jax import lax
from jax.experimental import pallas as pl
from jax.experimental.pallas import tpu as pltpu
from jax.sharding import PartitionSpec as P

MESH = pl.DeviceIdType.MESH
BF = jnp.bfloat16
F32 = jnp.float32
CHUNKS = 4
WAYS = ((1, 0), (-1, 1))


def place_of(dev, n):
    odd = lax.rem(dev, 2)
    half = lax.div(dev, 2)
    return (1 - odd) * half + odd * (n - 1 - half)


def dev_of(place, n):
    q = lax.rem(place + 2 * n, n)
    high = lax.div(q, n // 2)
    return (1 - high) * (2 * q) + high * (2 * (n - 1 - q) + 1)


def exchange(
    n,
    tenant_ref, rows_ref, owner_ref, in_hbm, cot_hbm, down_hbm, up_hbm,
    delta_hbm, gin_hbm, terms_hbm, slots_hbm,
    tokens, adapters, slot_src, slots, first, moving, mine, part_mine, part_other, ranks, terms,
    result,
    load_sem, slot_send, slot_recv, rs_send, rs_recv, part_send, part_recv,
    ag_send, ag_recv, keep_sem, out_sem, slot_out, credit,
):
    own, rank, width = down_hbm.shape
    half = width // 2
    depth = moving.shape[2]
    d = lax.axis_index("dp")
    t = lax.axis_index("tensor")
    p = place_of(d, n)
    neighbour = (dev_of(p + 1, n), dev_of(p - 1, n))

    loads = [
        pltpu.make_async_copy(down_hbm, adapters.at[0], load_sem.at[0]),
        pltpu.make_async_copy(up_hbm, adapters.at[1], load_sem.at[1]),
        pltpu.make_async_copy(in_hbm, tokens.at[0], load_sem.at[2]),
        pltpu.make_async_copy(cot_hbm, tokens.at[1], load_sem.at[3]),
    ]
    for load in loads:
        load.start()

    barrier = pltpu.get_barrier_semaphore()

    def greet(i, _):
        pl.semaphore_signal(
            barrier, inc=1, device_id={"dp": lax.rem(d + i, n)}, device_id_type=MESH
        )
        return 0

    lax.fori_loop(1, n, greet, 0)
    pl.semaphore_signal(barrier, inc=1, device_id={"tensor": 1 - t}, device_id_type=MESH)
    my_slot = owner_ref[tenant_ref[0]]
    slot_vec = jnp.full((1, 128), my_slot, jnp.int32)
    slot_src[...] = slot_vec
    slots[d] = slot_vec
    pl.semaphore_wait(barrier, n)

    def slot_copy(i):
        to = lax.rem(d + i, n)
        return pltpu.make_async_remote_copy(
            src_ref=slot_src, dst_ref=slots.at[d],
            send_sem=slot_send.at[i], recv_sem=slot_recv.at[d],
            device_id={"dp": to}, device_id_type=MESH,
        )

    def slot_wait(i):
        who = lax.rem(d + i, n)
        return pltpu.make_async_remote_copy(
            src_ref=slot_src, dst_ref=slots.at[who],
            send_sem=slot_send.at[i], recv_sem=slot_recv.at[who],
            device_id={"dp": who}, device_id_type=MESH,
        )

    lax.fori_loop(1, n, lambda i, c: (slot_copy(i).start(), c)[1], 0)
    loads[0].wait()
    loads[1].wait()
    lax.fori_loop(1, n, lambda i, c: (slot_wait(i).wait_recv(), c)[1], 0)

    def masks(block):
        v = jnp.broadcast_to(slots[block], (rank, 128))
        return [
            jnp.where(v == d * own + j, 1.0, 0.0).astype(F32).astype(BF) for j in range(own)
        ]

    def share(a, r, chosen):
        total = None
        for j in range(own):
            gate = jnp.concatenate([chosen[j]] * (half // 128), axis=1)
            term = gate * adapters[a, j, :, r * half:(r + 1) * half]
            total = term if total is None else total + term
        return total

    def rs_copy(a, r, step, src):
        return pltpu.make_async_remote_copy(
            src_ref=src, dst_ref=moving.at[a, r, lax.rem(step, depth)],
            send_sem=rs_send.at[a, r, lax.rem(step, depth)],
            recv_sem=rs_recv.at[a, r, lax.rem(step, depth)],
            device_id={"dp": neighbour[r]}, device_id_type=MESH,
        )

    def source(a, r, step):
        return moving.at[a, r, lax.rem(step - 1 + depth, depth)]

    for way, r in WAYS:
        chosen = masks(dev_of(p - way, n))
        for a in range(2):
            first[a, r] = share(a, r, chosen)
            rs_copy(a, r, 0, first.at[a, r]).start()

    def rs_step(step, _):
        chosen = [masks(dev_of(p - way * (1 + step), n)) for way, r in WAYS]
        for a in range(2):
            for way, r in WAYS:
                add = share(a, r, chosen[r])
                rs_copy(a, r, step - 1, first.at[a, r]).wait_recv()
                here = lax.rem(step - 1, depth)
                moving[a, r, here] = moving[a, r, here] + add
                if depth < n - 1:
                    rs_copy(a, r, step - 1, first.at[a, r]).wait_send()

                    @pl.when((step >= 2) & (step - 2 <= n - 2 - depth))
                    def _():
                        pl.semaphore_signal(
                            credit.at[a, r], inc=1,
                            device_id={"dp": neighbour[1 - r]}, device_id_type=MESH,
                        )

                    @pl.when(step >= depth)
                    def _():
                        pl.semaphore_wait(credit.at[a, r], 1)

                rs_copy(a, r, step, source(a, r, step)).start()
        return 0

    lax.fori_loop(1, n - 1, rs_step, 0)

    lanes = lax.broadcasted_iota(jnp.int32, (rank, 128), 1)
    keep = jnp.where(lanes < rows_ref[0], 1.0, 0.0).astype(F32)
    loads[2].wait()
    loads[3].wait()
    own_chosen = masks(d)

    def part_copy(a):
        return pltpu.make_async_remote_copy(
            src_ref=part_mine.at[a], dst_ref=part_other.at[a],
            send_sem=part_send.at[a], recv_sem=part_recv.at[a],
            device_id={"tensor": 1 - t}, device_id_type=MESH,
        )

    for a in range(2):
        for way, r in WAYS:
            add = share(a, r, own_chosen)
            rs_copy(a, r, n - 2, first.at[a, r]).wait_recv()
            mine[a, :, r * half:(r + 1) * half] = moving[a, r, (n - 2) % depth] + add
        part_mine[a] = jnp.dot(mine[a], tokens[a], preferred_element_type=F32)
        part_copy(a).start()

    def ag_copy(a, r, step):
        block = dev_of(p - WAYS[r][0] * step, n)
        piece = terms.at[a, block, :, pl.ds(r * half, half)]
        return pltpu.make_async_remote_copy(
            src_ref=piece, dst_ref=piece,
            send_sem=ag_send.at[a, r, step], recv_sem=ag_recv.at[a, r, step],
            device_id={"dp": neighbour[r]}, device_id_type=MESH,
        )

    def ag_arrive(a, r, step):
        block = dev_of(p - WAYS[r][0] * (step + 1), n)
        piece = terms.at[a, block, :, pl.ds(r * half, half)]
        return pltpu.make_async_remote_copy(
            src_ref=piece, dst_ref=piece,
            send_sem=ag_send.at[a, r, step], recv_sem=ag_recv.at[a, r, step],
            device_id={"dp": neighbour[r]}, device_id_type=MESH,
        )

    def keep_copy(a, r, step):
        block = dev_of(p - WAYS[r][0] * step, n)
        return pltpu.make_async_copy(
            terms.at[a, block, :, pl.ds(r * half, half)],
            terms_hbm.at[a, block, :, pl.ds(r * half, half)],
            keep_sem.at[a, r, step],
        )

    for a in range(2):
        part_copy(a).wait_recv()
        ranks[a] = ((part_mine[a] + part_other[a]) * keep).astype(BF)
        for r in range(2):
            terms[a, d, :, r * half:(r + 1) * half] = lax.dot_general(
                ranks[a], tokens[1 - a, r * half:(r + 1) * half, :],
                (((1,), (1,)), ((), ())), preferred_element_type=F32,
            ).astype(BF)
            ag_copy(a, r, 0).start()
            keep_copy(a, r, 0).start()

    size = width // CHUNKS

    def result_copy(a, i):
        at = pl.ds(i * size, size)
        return pltpu.make_async_copy(
            result.at[a, at], (delta_hbm, gin_hbm)[a].at[at], out_sem.at[a, i]
        )

    def result_chunk(i):
        at = slice(i * size, (i + 1) * size)
        for a in range(2):
            twice = ranks[a] + ranks[a]
            result[a, at, :] = lax.dot_general(
                mine[1 - a, :, at], twice,
                (((0,), (0,)), ((), ())), preferred_element_type=F32,
            ).astype(BF)
            result_copy(a, i).start()

    def ag_step(step):
        for a in range(2):
            for r in range(2):
                ag_arrive(a, r, step - 1).wait_recv()
                ag_copy(a, r, step).start()
                keep_copy(a, r, step).start()

    result_chunk(0)
    early = min(CHUNKS, n - 1)
    for step in range(1, early):
        ag_step(step)
        result_chunk(step)
    for i in range(early, CHUNKS):
        result_chunk(i)
    lax.fori_loop(early, n - 1, lambda s, c: (ag_step(s), c)[1], 0)
    slot_keep = pltpu.make_async_copy(slots, slots_hbm, slot_out)
    slot_keep.start()
    for a in range(2):
        for r in range(2):
            ag_arrive(a, r, n - 2).wait_recv()
            keep_copy(a, r, n - 1).start()

    def slot_end(i, c):
        slot_copy(i).wait_send()
        return c

    lax.fori_loop(1, n, slot_end, 0)

    def rs_end(step, c):
        for a in range(2):
            for r in range(2):
                rs_copy(a, r, step, first.at[a, r]).wait_send()
        return c

    lax.fori_loop(n - 2 if depth < n - 1 else 0, n - 1, rs_end, 0)

    def ag_end(step, c):
        for a in range(2):
            for r in range(2):
                ag_copy(a, r, step).wait_send()
        return c

    lax.fori_loop(0, n - 1, ag_end, 0)

    def keep_end(step, c):
        for a in range(2):
            for r in range(2):
                keep_copy(a, r, step).wait()
        return c

    lax.fori_loop(0, n, keep_end, 0)
    for a in range(2):
        part_copy(a).wait_send()
        for i in range(CHUNKS):
            result_copy(a, i).wait()
    slot_keep.wait()


def collect(n, slots_ref, base_ref, terms_ref, down_ref, up_ref):
    own = down_ref.shape[0]
    down_ref[...] = jnp.zeros_like(down_ref)
    up_ref[...] = jnp.zeros_like(up_ref)

    def add(b, c):
        at = slots_ref[b, 0, 0] - base_ref[0]

        @pl.when((at >= 0) & (at < own))
        def _():
            up_ref[at] += 0.125 * terms_ref[0, b].astype(F32)
            down_ref[at] += 0.125 * terms_ref[1, b].astype(F32)

        return c

    lax.fori_loop(0, n, add, 0)


def shards(n, inputs_t, cotangent_t, adapter_down, adapter_up, block_tenant, block_rows, owner_slot):
    width, columns = inputs_t.shape
    own, rank, _ = adapter_down.shape
    half = width // 2
    depth = min(n - 1, 8)
    smem = pl.BlockSpec(memory_space=pltpu.SMEM)
    anyw = pl.BlockSpec(memory_space=pl.ANY)
    dma = pltpu.SemaphoreType.DMA
    delta_t, grad_input_t, terms, slots = pl.pallas_call(
        functools.partial(exchange, n),
        out_shape=(
            jax.ShapeDtypeStruct((width, columns), BF),
            jax.ShapeDtypeStruct((width, columns), BF),
            jax.ShapeDtypeStruct((2, n, rank, width), BF),
            jax.ShapeDtypeStruct((n, 1, 128), jnp.int32),
        ),
        in_specs=[smem, smem, smem, anyw, anyw, anyw, anyw],
        out_specs=(anyw,) * 4,
        scratch_shapes=[
            pltpu.VMEM((2, width, columns), BF),
            pltpu.VMEM((2, own, rank, width), BF),
            pltpu.VMEM((1, 128), jnp.int32),
            pltpu.VMEM((n, 1, 128), jnp.int32),
            pltpu.VMEM((2, 2, rank, half), BF),
            pltpu.VMEM((2, 2, depth, rank, half), BF),
            pltpu.VMEM((2, rank, width), BF),
            pltpu.VMEM((2, rank, columns), F32),
            pltpu.VMEM((2, rank, columns), F32),
            pltpu.VMEM((2, rank, columns), BF),
            pltpu.VMEM((2, n, rank, width), BF),
            pltpu.VMEM((2, width, columns), BF),
            dma((4,)),
            dma((n,)),
            dma((n,)),
            dma((2, 2, depth)),
            dma((2, 2, depth)),
            dma((2,)),
            dma((2,)),
            dma((2, 2, n)),
            dma((2, 2, n)),
            dma((2, 2, n)),
            dma((2, CHUNKS)),
            dma,
            pltpu.SemaphoreType.REGULAR((2, 2)),
        ],
        compiler_params=pltpu.CompilerParams(
            collective_id=0, has_side_effects=True, vmem_limit_bytes=56 * 1024 * 1024
        ),
        name="exchange",
    )(block_tenant, block_rows, owner_slot, inputs_t, cotangent_t, adapter_down, adapter_up)
    base = jnp.full((1,), lax.axis_index("dp") * own, jnp.int32)
    tile = min(width, 512)
    grad_down, grad_up = pl.pallas_call(
        functools.partial(collect, n),
        grid=(width // tile,),
        out_shape=(
            jax.ShapeDtypeStruct((own, rank, width), F32),
            jax.ShapeDtypeStruct((own, rank, width), F32),
        ),
        in_specs=[smem, smem, pl.BlockSpec((2, n, rank, tile), lambda i: (0, 0, 0, i))],
        out_specs=(
            pl.BlockSpec((own, rank, tile), lambda i: (0, 0, i)),
            pl.BlockSpec((own, rank, tile), lambda i: (0, 0, i)),
        ),
        compiler_params=pltpu.CompilerParams(vmem_limit_bytes=40 * 1024 * 1024),
        name="collect",
    )(slots, base, terms)
    return delta_t, grad_input_t, grad_down, grad_up


def solution(mesh):
    return jax.shard_map(
        functools.partial(shards, mesh.shape["dp"]),
        mesh=mesh,
        in_specs=(
            P("tensor", ("groups", "dp")),
            P("tensor", ("groups", "dp")),
            P(("groups", "dp"), None, "tensor"),
            P(("groups", "dp"), None, "tensor"),
            P(("groups", "dp")),
            P(("groups", "dp")),
            P("groups"),
        ),
        out_specs=(
            P("tensor", ("groups", "dp")),
            P("tensor", ("groups", "dp")),
            P(("groups", "dp"), None, "tensor"),
            P(("groups", "dp"), None, "tensor"),
        ),
        check_vma=False,
    )
```

time: 315 us -> 77.9 us (0.25)
  local copies, waits for them, and re-layouts: 103 us -> 4.2 us
  waiting for transfers between devices: 94.1 us -> 0 us
  Pallas kernels: 0 us -> 71.5 us
  other arithmetic: 42.8 us -> 0 us
  starting transfers between devices: 40.2 us -> 0 us
  blocking collectives: 26.2 us -> 0 us
  matrix products: 4.98 us -> 0 us
    all_to_all x8 -> x0, waiting for transfers between devices: 94.1 us -> none  [the longest x1 41.7 us: shards(): lax.all_to_all(grad_scale * sum_up, 'dp', split_axis=0, concat_axis=2, ti...]
    pallas_call x0 -> x2, Pallas kernels: none -> 71.5 us  [the longest x1 66.8 us: shards(): pl.pallas_call(functools.partial(exchange, n), out_shape=(jax.ShapeDtypeS...]
    unnamed x30 -> x10, local copies, waits for them, and re-layouts: 72.2 us -> 4.2 us
    all_to_all x8 -> x0, starting transfers between devices: 40.2 us -> none  [the longest x1 7.38 us: shards(): lax.all_to_all(adapter_up, 'dp', split_axis=2, concat_axis=0, tiled=True)]
    unnamed x2 -> x0, other arithmetic: 38.7 us -> none
    all_to_all x6 -> x0, local copies, waits for them, and re-layouts: 24.2 us -> none  [the longest x1 9.13 us: shards(): lax.all_to_all(adapter_up, 'dp', split_axis=2, concat_axis=0, tiled=True)]
    unnamed x1 -> x0, blocking collectives: 22.8 us -> none
    mul x2 -> x0, local copies, waits for them, and re-layouts: 5.06 us -> none  [the longest x1 2.54 us: shards(): grad_scale * sum_down]
  transfers between devices with their start and end apart: 8 -> 0, of which waited for: 4 -> 0; matrix products, arithmetic and copies ran while one was open for 34% -> 0% of each run, Pallas kernels for 0% -> 0%
where the time goes in v1:
time: 77.9 us; the launch traced here: 77.7 us
  Pallas kernels  71.5 us (92%)
  local copies, waits for them, and re-layouts  4.2 us (5%)
  between operations  1.95 us (3%)
    pallas_call x1, Pallas kernels, shards(): pl.pallas_call(functools.partial(exchange, n), out_shape=(jax.ShapeDtypeS...  66.8 us
    pallas_call x1, Pallas kernels, shards(): pl.pallas_call(functools.partial(collect, n), grid=(width // tile,), out_...  4.69 us
    unnamed x10, local copies, waits for them, and re-layouts  4.2 us

profile of v1, /device:TPU:0, one launch (start us, length us, event | category | flops | bytes accessed | tf_op | source)
XLA Modules:
  0.0 77.7 jit_solution(5325386096375823361)
XLA Ops:
  1.9 66.8 %exchange.1 = (bf16[4096,128]{1,0:T(8,128)(2,1)}, bf16[4096,128]{1,0:T(8,128)(2,1)}, bf16[2,8,16,4096]{3,2,1,0:T(8,128)(2,1)}, s32[8,1,128]{2,1,0:T(1,128)}) custom-call(s32[1]{0:T(128)S(6)} %copy.13.tenant_ref, s32[1]{0:T(128)S(6)} %copy.14.rows_ref, s32[64]{0:T(128)} %owner_ref.1, bf16[4096,128]{1,0:T(8,128)(2,1)} %in_hbm.1, bf16[4096,128]{1,0:T(8,128)(2,1)} %cot_hbm.1, ...), custom_call_target="tpu_custom_call" | custom-call | tf_op jit(solution)/shard_map/exchange/pallas_call | solution.py:309
  68.8 0.0 copy-start
  68.8 1.6 %copy-done = bf16[2,8,16,4096]{3,2,1,0:T(8,128)(2,1)S(1)} copy-done((bf16[2,8,16,4096]{3,2,1,0:T(8,128)(2,1)S(1)}, bf16[2,8,16,4096]{3,2,1,0:T(8,128)(2,1)}, u32[]{:S(2)}) %copy-start) | copy-done | bytes 2097176
  70.3 0.0 copy-start.1
  70.3 0.7 copy-done.1
  71.0 0.0 copy-start.3
  71.0 0.0 copy-start.2
  71.0 4.7 %collect.1 = (f32[8,16,4096]{2,1,0:T(8,128)}, f32[8,16,4096]{2,1,0:T(8,128)}) custom-call(s32[8,1,128]{2,1,0:T(1,128)S(1)} %copy-done.1, s32[1]{0:T(128)} %bitcast.base_ref, bf16[2,8,16,4096]{3,2,1,0:T(8,128)(2,1)S(1)} %copy-done), custom_call_target="tpu_custom_call" | custom-call | tf_op jit(solution)/shard_map/collect/pallas_call | solution.py:353
  75.7 0.0 copy-done.3
  75.7 1.0 %copy.15 = bf16[4096,128]{1,0:T(8,128)(2,1)} copy(bf16[4096,128]{1,0:T(8,128)(2,1)S(1)} %copy-done.3) | data formatting | bytes 2097152
  76.7 0.0 copy-done.2
  76.7 1.0 %copy.16 = bf16[4096,128]{1,0:T(8,128)(2,1)} copy(bf16[4096,128]{1,0:T(8,128)(2,1)S(1)} %copy-done.2) | data formatting | bytes 2097152
Async XLA Ops:
  68.8 1.6 %copy-start = (bf16[2,8,16,4096]{3,2,1,0:T(8,128)(2,1)S(1)}, bf16[2,8,16,4096]{3,2,1,0:T(8,128)(2,1)}, u32[]{:S(2)}) copy-start(bf16[2,8,16,4096]{3,2,1,0:T(8,128)(2,1)} %get-tuple-element.13.terms_ref) | copy-start | bytes 6291460
  70.3 0.7 copy-start.1
  71.0 4.7 %copy-start.3 = (bf16[4096,128]{1,0:T(8,128)(2,1)S(1)}, bf16[4096,128]{1,0:T(8,128)(2,1)}, u32[]{:S(2)}) copy-start(bf16[4096,128]{1,0:T(8,128)(2,1)} %get-tuple-element.20) | copy-start | bytes 3145732
  71.0 5.7 %copy-start.2 = (bf16[4096,128]{1,0:T(8,128)(2,1)S(1)}, bf16[4096,128]{1,0:T(8,128)(2,1)}, u32[]{:S(2)}) copy-start(bf16[4096,128]{1,0:T(8,128)(2,1)} %get-tuple-element.21) | copy-start | bytes 3145732

commit v2 on v1

--- a/solution.py
+++ b/solution.py
@@ -10,7 +10,8 @@
 BF = jnp.bfloat16
 F32 = jnp.float32
 CHUNKS = 4
-WAYS = ((1, 0), (-1, 1))
+LANES = 4
+WAYS = tuple(1 if w < LANES // 2 else -1 for w in range(LANES))
 
 
 def place_of(dev, n):
@@ -29,13 +30,14 @@
     n,
     tenant_ref, rows_ref, owner_ref, in_hbm, cot_hbm, down_hbm, up_hbm,
     delta_hbm, gin_hbm, terms_hbm, slots_hbm,
-    tokens, adapters, slot_src, slots, first, moving, mine, part_mine, part_other, ranks, terms,
+    tokens, adapters, slot_src, slots, first, ready, moving, mine, part_mine, part_other, ranks, terms,
     result,
     load_sem, slot_send, slot_recv, rs_send, rs_recv, part_send, part_recv,
     ag_send, ag_recv, keep_sem, out_sem, slot_out, credit,
 ):
     own, rank, width = down_hbm.shape
     half = width // 2
+    piece = width // LANES
     depth = moving.shape[2]
     d = lax.axis_index("dp")
     t = lax.axis_index("tensor")
@@ -94,54 +96,64 @@
             jnp.where(v == d * own + j, 1.0, 0.0).astype(F32).astype(BF) for j in range(own)
         ]
 
-    def share(a, r, chosen):
+    def cut(w):
+        return slice(w * piece, (w + 1) * piece)
+
+    def share(a, w, chosen):
         total = None
         for j in range(own):
-            gate = jnp.concatenate([chosen[j]] * (half // 128), axis=1)
-            term = gate * adapters[a, j, :, r * half:(r + 1) * half]
+            gate = jnp.concatenate([chosen[j]] * (piece // 128), axis=1)
+            term = gate * adapters[a, j, :, cut(w)]
             total = term if total is None else total + term
         return total
 
-    def rs_copy(a, r, step, src):
-        return pltpu.make_async_remote_copy(
-            src_ref=src, dst_ref=moving.at[a, r, lax.rem(step, depth)],
-            send_sem=rs_send.at[a, r, lax.rem(step, depth)],
-            recv_sem=rs_recv.at[a, r, lax.rem(step, depth)],
-            device_id={"dp": neighbour[r]}, device_id_type=MESH,
-        )
-
-    def source(a, r, step):
-        return moving.at[a, r, lax.rem(step - 1 + depth, depth)]
-
-    for way, r in WAYS:
-        chosen = masks(dev_of(p - way, n))
-        for a in range(2):
-            first[a, r] = share(a, r, chosen)
-            rs_copy(a, r, 0, first.at[a, r]).start()
+    def prepare(step):
+        blocks = [dev_of(p - way * (1 + step), n) for way in (1, -1)]
+        chosen = [masks(block) for block in blocks]
+        for a in range(2):
+            for w in range(LANES):
+                ready[a, w] = share(a, w, chosen[(1 - WAYS[w]) // 2])
+
+    def target(w):
+        return neighbour[(1 - WAYS[w]) // 2]
+
+    def rs_copy(a, w, step, src):
+        return pltpu.make_async_remote_copy(
+            src_ref=src, dst_ref=moving.at[a, w, lax.rem(step, depth)],
+            send_sem=rs_send.at[a, w, lax.rem(step, depth)],
+            recv_sem=rs_recv.at[a, w, lax.rem(step, depth)],
+            device_id={"dp": target(w)}, device_id_type=MESH,
+        )
+
+    for a in range(2):
+        chosen = [masks(dev_of(p - way, n)) for way in (1, -1)]
+        for w in range(LANES):
+            first[a, w] = share(a, w, chosen[(1 - WAYS[w]) // 2])
+            rs_copy(a, w, 0, first.at[a, w]).start()
+    prepare(1)
 
     def rs_step(step, _):
-        chosen = [masks(dev_of(p - way * (1 + step), n)) for way, r in WAYS]
-        for a in range(2):
-            for way, r in WAYS:
-                add = share(a, r, chosen[r])
-                rs_copy(a, r, step - 1, first.at[a, r]).wait_recv()
-                here = lax.rem(step - 1, depth)
-                moving[a, r, here] = moving[a, r, here] + add
+        here = lax.rem(step - 1, depth)
+        for a in range(2):
+            for w in range(LANES):
+                rs_copy(a, w, step - 1, first.at[a, w]).wait_recv()
+                moving[a, w, here] = moving[a, w, here] + ready[a, w]
                 if depth < n - 1:
-                    rs_copy(a, r, step - 1, first.at[a, r]).wait_send()
+                    rs_copy(a, w, step - 1, first.at[a, w]).wait_send()
 
                     @pl.when((step >= 2) & (step - 2 <= n - 2 - depth))
                     def _():
                         pl.semaphore_signal(
-                            credit.at[a, r], inc=1,
-                            device_id={"dp": neighbour[1 - r]}, device_id_type=MESH,
+                            credit.at[a, w], inc=1,
+                            device_id={"dp": neighbour[(1 + WAYS[w]) // 2]}, device_id_type=MESH,
                         )
 
                     @pl.when(step >= depth)
                     def _():
-                        pl.semaphore_wait(credit.at[a, r], 1)
-
-                rs_copy(a, r, step, source(a, r, step)).start()
+                        pl.semaphore_wait(credit.at[a, w], 1)
+
+                rs_copy(a, w, step, moving.at[a, w, here]).start()
+        prepare(step + 1)
         return 0
 
     lax.fori_loop(1, n - 1, rs_step, 0)
@@ -150,7 +162,6 @@
     keep = jnp.where(lanes < rows_ref[0], 1.0, 0.0).astype(F32)
     loads[2].wait()
     loads[3].wait()
-    own_chosen = masks(d)
 
     def part_copy(a):
         return pltpu.make_async_remote_copy(
@@ -160,33 +171,35 @@
         )
 
     for a in range(2):
-        for way, r in WAYS:
-            add = share(a, r, own_chosen)
-            rs_copy(a, r, n - 2, first.at[a, r]).wait_recv()
-            mine[a, :, r * half:(r + 1) * half] = moving[a, r, (n - 2) % depth] + add
+        for w in range(LANES):
+            rs_copy(a, w, n - 2, first.at[a, w]).wait_recv()
+            mine[a, :, cut(w)] = moving[a, w, (n - 2) % depth] + ready[a, w]
         part_mine[a] = jnp.dot(mine[a], tokens[a], preferred_element_type=F32)
         part_copy(a).start()
 
-    def ag_copy(a, r, step):
-        block = dev_of(p - WAYS[r][0] * step, n)
-        piece = terms.at[a, block, :, pl.ds(r * half, half)]
-        return pltpu.make_async_remote_copy(
-            src_ref=piece, dst_ref=piece,
-            send_sem=ag_send.at[a, r, step], recv_sem=ag_recv.at[a, r, step],
-            device_id={"dp": neighbour[r]}, device_id_type=MESH,
-        )
-
-    def ag_arrive(a, r, step):
-        block = dev_of(p - WAYS[r][0] * (step + 1), n)
-        piece = terms.at[a, block, :, pl.ds(r * half, half)]
-        return pltpu.make_async_remote_copy(
-            src_ref=piece, dst_ref=piece,
-            send_sem=ag_send.at[a, r, step], recv_sem=ag_recv.at[a, r, step],
-            device_id={"dp": neighbour[r]}, device_id_type=MESH,
+    def ag_piece(a, w, step):
+        block = dev_of(p - WAYS[w] * step, n)
+        held = terms.at[a, block, :, pl.ds(w * piece, piece)]
+        return held
+
+    def ag_copy(a, w, step):
+        held = ag_piece(a, w, step)
+        return pltpu.make_async_remote_copy(
+            src_ref=held, dst_ref=held,
+            send_sem=ag_send.at[a, w, step], recv_sem=ag_recv.at[a, w, step],
+            device_id={"dp": target(w)}, device_id_type=MESH,
+        )
+
+    def ag_arrive(a, w, step):
+        held = ag_piece(a, w, step + 1)
+        return pltpu.make_async_remote_copy(
+            src_ref=held, dst_ref=held,
+            send_sem=ag_send.at[a, w, step], recv_sem=ag_recv.at[a, w, step],
+            device_id={"dp": target(w)}, device_id_type=MESH,
         )
 
     def keep_copy(a, r, step):
-        block = dev_of(p - WAYS[r][0] * step, n)
+        block = dev_of(p - (1 - 2 * r) * step, n)
         return pltpu.make_async_copy(
             terms.at[a, block, :, pl.ds(r * half, half)],
             terms_hbm.at[a, block, :, pl.ds(r * half, half)],
@@ -196,12 +209,13 @@
     for a in range(2):
         part_copy(a).wait_recv()
         ranks[a] = ((part_mine[a] + part_other[a]) * keep).astype(BF)
-        for r in range(2):
-            terms[a, d, :, r * half:(r + 1) * half] = lax.dot_general(
-                ranks[a], tokens[1 - a, r * half:(r + 1) * half, :],
+        for w in range(LANES):
+            terms[a, d, :, cut(w)] = lax.dot_general(
+                ranks[a], tokens[1 - a, cut(w), :],
                 (((1,), (1,)), ((), ())), preferred_element_type=F32,
             ).astype(BF)
-            ag_copy(a, r, 0).start()
+            ag_copy(a, w, 0).start()
+        for r in range(2):
             keep_copy(a, r, 0).start()
 
     size = width // CHUNKS
@@ -224,9 +238,10 @@
 
     def ag_step(step):
         for a in range(2):
+            for w in range(LANES):
+                ag_arrive(a, w, step - 1).wait_recv()
+                ag_copy(a, w, step).start()
             for r in range(2):
-                ag_arrive(a, r, step - 1).wait_recv()
-                ag_copy(a, r, step).start()
                 keep_copy(a, r, step).start()
 
     result_chunk(0)
@@ -240,8 +255,9 @@
     slot_keep = pltpu.make_async_copy(slots, slots_hbm, slot_out)
     slot_keep.start()
     for a in range(2):
+        for w in range(LANES):
+            ag_arrive(a, w, n - 2).wait_recv()
         for r in range(2):
-            ag_arrive(a, r, n - 2).wait_recv()
             keep_copy(a, r, n - 1).start()
 
     def slot_end(i, c):
@@ -252,16 +268,16 @@
 
     def rs_end(step, c):
         for a in range(2):
-            for r in range(2):
-                rs_copy(a, r, step, first.at[a, r]).wait_send()
+            for w in range(LANES):
+                rs_copy(a, w, step, first.at[a, w]).wait_send()
         return c
 
     lax.fori_loop(n - 2 if depth < n - 1 else 0, n - 1, rs_end, 0)
 
     def ag_end(step, c):
         for a in range(2):
-            for r in range(2):
-                ag_copy(a, r, step).wait_send()
+            for w in range(LANES):
+                ag_copy(a, w, step).wait_send()
         return c
 
     lax.fori_loop(0, n - 1, ag_end, 0)
@@ -301,7 +317,7 @@
 def shards(n, inputs_t, cotangent_t, adapter_down, adapter_up, block_tenant, block_rows, owner_slot):
     width, columns = inputs_t.shape
     own, rank, _ = adapter_down.shape
-    half = width // 2
+    piece = width // LANES
     depth = min(n - 1, 8)
     smem = pl.BlockSpec(memory_space=pltpu.SMEM)
     anyw = pl.BlockSpec(memory_space=pl.ANY)
@@ -321,8 +337,9 @@
             pltpu.VMEM((2, own, rank, width), BF),
             pltpu.VMEM((1, 128), jnp.int32),
             pltpu.VMEM((n, 1, 128), jnp.int32),
-            pltpu.VMEM((2, 2, rank, half), BF),
-            pltpu.VMEM((2, 2, depth, rank, half), BF),
+            pltpu.VMEM((2, LANES, rank, piece), BF),
+            pltpu.VMEM((2, LANES, rank, piece), BF),
+            pltpu.VMEM((2, LANES, depth, rank, piece), BF),
             pltpu.VMEM((2, rank, width), BF),
             pltpu.VMEM((2, rank, columns), F32),
             pltpu.VMEM((2, rank, columns), F32),
@@ -332,16 +349,16 @@
             dma((4,)),
             dma((n,)),
             dma((n,)),
-            dma((2, 2, depth)),
-            dma((2, 2, depth)),
+            dma((2, LANES, depth)),
+            dma((2, LANES, depth)),
             dma((2,)),
             dma((2,)),
-            dma((2, 2, n)),
-            dma((2, 2, n)),
+            dma((2, LANES, n)),
+            dma((2, LANES, n)),
             dma((2, 2, n)),
             dma((2, CHUNKS)),
             dma,
-            pltpu.SemaphoreType.REGULAR((2, 2)),
+            pltpu.SemaphoreType.REGULAR((2, LANES)),
         ],
         compiler_params=pltpu.CompilerParams(
             collective_id=0, has_side_effects=True, vmem_limit_bytes=56 * 1024 * 1024
@@ -349,7 +366,7 @@
         name="exchange",
     )(block_tenant, block_rows, owner_slot, inputs_t, cotangent_t, adapter_down, adapter_up)
     base = jnp.full((1,), lax.axis_index("dp") * own, jnp.int32)
-    tile = min(width, 512)
+    tile = min(width, 1024)
     grad_down, grad_up = pl.pallas_call(
         functools.partial(collect, n),
         grid=(width // tile,),
@@ -362,7 +379,7 @@
             pl.BlockSpec((own, rank, tile), lambda i: (0, 0, i)),
             pl.BlockSpec((own, rank, tile), lambda i: (0, 0, i)),
         ),
-        compiler_params=pltpu.CompilerParams(vmem_limit_bytes=40 * 1024 * 1024),
+        compiler_params=pltpu.CompilerParams(vmem_limit_bytes=60 * 1024 * 1024),
         name="collect",
     )(slots, base, terms)
     return delta_t, grad_input_t, grad_down, grad_up

time: 77.9 us -> 72.1 us (0.926)
  Pallas kernels: 71.5 us -> 68 us
  local copies, waits for them, and re-layouts: 4.2 us -> 1.95 us
    pallas_call x1, Pallas kernels: 66.8 us -> 63.4 us  [shards(): pl.pallas_call(functools.partial(exchange, n), out_shape=(jax.ShapeDtypeS...]
    unnamed x10 -> x6, local copies, waits for them, and re-layouts: 4.2 us -> 1.95 us
where the time goes in v2:
time: 72.1 us; the launch traced here: 71.9 us
  Pallas kernels  68 us (94%)
  local copies, waits for them, and re-layouts  1.95 us (3%)
  between operations  1.95 us (3%)
    pallas_call x1, Pallas kernels, shards(): pl.pallas_call(functools.partial(exchange, n), out_shape=(jax.ShapeDtypeS...  63.4 us
    pallas_call x1, Pallas kernels, shards(): pl.pallas_call(functools.partial(collect, n), grid=(width // tile,), out_...  4.64 us
    unnamed x6, local copies, waits for them, and re-layouts  1.95 us

profile of v2, /device:TPU:0, one launch (start us, length us, event | category | flops | bytes accessed | tf_op | source)
XLA Modules:
  0.0 71.9 jit_solution(13210299392568953510)
XLA Ops:
  1.9 63.4 %exchange.1 = (bf16[4096,128]{1,0:T(8,128)(2,1)}, bf16[4096,128]{1,0:T(8,128)(2,1)}, bf16[2,8,16,4096]{3,2,1,0:T(8,128)(2,1)}, s32[8,1,128]{2,1,0:T(1,128)}) custom-call(s32[1]{0:T(128)S(6)} %copy.13.tenant_ref, s32[1]{0:T(128)S(6)} %copy.14.rows_ref, s32[64]{0:T(128)} %owner_ref.1, bf16[4096,128]{1,0:T(8,128)(2,1)} %in_hbm.1, bf16[4096,128]{1,0:T(8,128)(2,1)} %cot_hbm.1, ...), custom_call_target="tpu_custom_call" | custom-call | tf_op jit(solution)/shard_map/exchange/pallas_call | solution.py:325
  65.3 0.0 copy-start.1
  65.3 0.0 copy-start
  65.3 4.6 %collect.1 = (f32[8,16,4096]{2,1,0:T(8,128)}, f32[8,16,4096]{2,1,0:T(8,128)}) custom-call(s32[8,1,128]{2,1,0:T(1,128)} %get-tuple-element.12.slots_ref, s32[1]{0:T(128)} %bitcast.base_ref, bf16[2,8,16,4096]{3,2,1,0:T(8,128)(2,1)} %get-tuple-element.13.terms_ref), custom_call_target="tpu_custom_call" | custom-call | tf_op jit(solution)/shard_map/collect/pallas_call | solution.py:370
  70.0 0.0 copy-done.1
  70.0 1.0 %copy.15 = bf16[4096,128]{1,0:T(8,128)(2,1)} copy(bf16[4096,128]{1,0:T(8,128)(2,1)S(1)} %copy-done.1) | data formatting | bytes 2097152
  70.9 0.0 copy-done
  70.9 1.0 %copy.16 = bf16[4096,128]{1,0:T(8,128)(2,1)} copy(bf16[4096,128]{1,0:T(8,128)(2,1)S(1)} %copy-done) | data formatting | bytes 2097152
Async XLA Ops:
  65.3 4.7 %copy-start.1 = (bf16[4096,128]{1,0:T(8,128)(2,1)S(1)}, bf16[4096,128]{1,0:T(8,128)(2,1)}, u32[]{:S(2)}) copy-start(bf16[4096,128]{1,0:T(8,128)(2,1)} %get-tuple-element.20) | copy-start | bytes 3145732
  65.3 5.6 %copy-start = (bf16[4096,128]{1,0:T(8,128)(2,1)S(1)}, bf16[4096,128]{1,0:T(8,128)(2,1)}, u32[]{:S(2)}) copy-start(bf16[4096,128]{1,0:T(8,128)(2,1)} %get-tuple-element.21) | copy-start | bytes 3145732

commit v3 on v2

--- a/solution.py
+++ b/solution.py
@@ -9,7 +9,6 @@
 MESH = pl.DeviceIdType.MESH
 BF = jnp.bfloat16
 F32 = jnp.float32
-CHUNKS = 4
 LANES = 4
 WAYS = tuple(1 if w < LANES // 2 else -1 for w in range(LANES))
 
@@ -29,11 +28,10 @@
 def exchange(
     n,
     tenant_ref, rows_ref, owner_ref, in_hbm, cot_hbm, down_hbm, up_hbm,
-    delta_hbm, gin_hbm, terms_hbm, slots_hbm,
+    mine_hbm, ranks_hbm, terms_hbm, slots_hbm,
     tokens, adapters, slot_src, slots, first, ready, moving, mine, part_mine, part_other, ranks, terms,
-    result,
     load_sem, slot_send, slot_recv, rs_send, rs_recv, part_send, part_recv,
-    ag_send, ag_recv, keep_sem, out_sem, slot_out, credit,
+    ag_send, ag_recv, keep_sem, out_sem, credit,
 ):
     own, rank, width = down_hbm.shape
     half = width // 2
@@ -173,8 +171,10 @@
     for a in range(2):
         for w in range(LANES):
             rs_copy(a, w, n - 2, first.at[a, w]).wait_recv()
-            mine[a, :, cut(w)] = moving[a, w, (n - 2) % depth] + ready[a, w]
-        part_mine[a] = jnp.dot(mine[a], tokens[a], preferred_element_type=F32)
+            got = moving[a, w, (n - 2) % depth] + ready[a, w]
+            mine[a, :, cut(w)] = got
+            term = jnp.dot(got, tokens[a, cut(w), :], preferred_element_type=F32)
+            part_mine[a] = term if w == 0 else part_mine[a] + term
         part_copy(a).start()
 
     def ag_piece(a, w, step):
@@ -218,23 +218,13 @@
         for r in range(2):
             keep_copy(a, r, 0).start()
 
-    size = width // CHUNKS
-
-    def result_copy(a, i):
-        at = pl.ds(i * size, size)
-        return pltpu.make_async_copy(
-            result.at[a, at], (delta_hbm, gin_hbm)[a].at[at], out_sem.at[a, i]
-        )
-
-    def result_chunk(i):
-        at = slice(i * size, (i + 1) * size)
-        for a in range(2):
-            twice = ranks[a] + ranks[a]
-            result[a, at, :] = lax.dot_general(
-                mine[1 - a, :, at], twice,
-                (((0,), (0,)), ((), ())), preferred_element_type=F32,
-            ).astype(BF)
-            result_copy(a, i).start()
+    outs = [
+        pltpu.make_async_copy(mine, mine_hbm, out_sem.at[0]),
+        pltpu.make_async_copy(ranks, ranks_hbm, out_sem.at[1]),
+        pltpu.make_async_copy(slots, slots_hbm, out_sem.at[2]),
+    ]
+    for out in outs:
+        out.start()
 
     def ag_step(step):
         for a in range(2):
@@ -244,16 +234,7 @@
             for r in range(2):
                 keep_copy(a, r, step).start()
 
-    result_chunk(0)
-    early = min(CHUNKS, n - 1)
-    for step in range(1, early):
-        ag_step(step)
-        result_chunk(step)
-    for i in range(early, CHUNKS):
-        result_chunk(i)
-    lax.fori_loop(early, n - 1, lambda s, c: (ag_step(s), c)[1], 0)
-    slot_keep = pltpu.make_async_copy(slots, slots_hbm, slot_out)
-    slot_keep.start()
+    lax.fori_loop(1, n - 1, lambda k, c: (ag_step(k), c)[1], 0)
     for a in range(2):
         for w in range(LANES):
             ag_arrive(a, w, n - 2).wait_recv()
@@ -291,12 +272,13 @@
     lax.fori_loop(0, n, keep_end, 0)
     for a in range(2):
         part_copy(a).wait_send()
-        for i in range(CHUNKS):
-            result_copy(a, i).wait()
-    slot_keep.wait()
-
-
-def collect(n, slots_ref, base_ref, terms_ref, down_ref, up_ref):
+    for out in outs:
+        out.wait()
+
+
+def collect(
+    n, slots_ref, base_ref, terms_ref, mine_ref, ranks_ref, delta_ref, gin_ref, down_ref, up_ref
+):
     own = down_ref.shape[0]
     down_ref[...] = jnp.zeros_like(down_ref)
     up_ref[...] = jnp.zeros_like(up_ref)
@@ -312,6 +294,11 @@
         return c
 
     lax.fori_loop(0, n, add, 0)
+    for a, out in enumerate((delta_ref, gin_ref)):
+        out[...] = lax.dot_general(
+            mine_ref[1 - a], ranks_ref[a] + ranks_ref[a],
+            (((0,), (0,)), ((), ())), preferred_element_type=F32,
+        ).astype(BF)
 
 
 def shards(n, inputs_t, cotangent_t, adapter_down, adapter_up, block_tenant, block_rows, owner_slot):
@@ -322,11 +309,11 @@
     smem = pl.BlockSpec(memory_space=pltpu.SMEM)
     anyw = pl.BlockSpec(memory_space=pl.ANY)
     dma = pltpu.SemaphoreType.DMA
-    delta_t, grad_input_t, terms, slots = pl.pallas_call(
+    mine, ranks, terms, slots = pl.pallas_call(
         functools.partial(exchange, n),
         out_shape=(
-            jax.ShapeDtypeStruct((width, columns), BF),
-            jax.ShapeDtypeStruct((width, columns), BF),
+            jax.ShapeDtypeStruct((2, rank, width), BF),
+            jax.ShapeDtypeStruct((2, rank, columns), BF),
             jax.ShapeDtypeStruct((2, n, rank, width), BF),
             jax.ShapeDtypeStruct((n, 1, 128), jnp.int32),
         ),
@@ -345,7 +332,6 @@
             pltpu.VMEM((2, rank, columns), F32),
             pltpu.VMEM((2, rank, columns), BF),
             pltpu.VMEM((2, n, rank, width), BF),
-            pltpu.VMEM((2, width, columns), BF),
             dma((4,)),
             dma((n,)),
             dma((n,)),
@@ -356,8 +342,7 @@
             dma((2, LANES, n)),
             dma((2, LANES, n)),
             dma((2, 2, n)),
-            dma((2, CHUNKS)),
-            dma,
+            dma((3,)),
             pltpu.SemaphoreType.REGULAR((2, LANES)),
         ],
         compiler_params=pltpu.CompilerParams(
@@ -366,23 +351,32 @@
         name="exchange",
     )(block_tenant, block_rows, owner_slot, inputs_t, cotangent_t, adapter_down, adapter_up)
     base = jnp.full((1,), lax.axis_index("dp") * own, jnp.int32)
-    tile = min(width, 1024)
-    grad_down, grad_up = pl.pallas_call(
+    tile = min(width, 2048)
+    return pl.pallas_call(
         functools.partial(collect, n),
         grid=(width // tile,),
         out_shape=(
+            jax.ShapeDtypeStruct((width, columns), BF),
+            jax.ShapeDtypeStruct((width, columns), BF),
             jax.ShapeDtypeStruct((own, rank, width), F32),
             jax.ShapeDtypeStruct((own, rank, width), F32),
         ),
-        in_specs=[smem, smem, pl.BlockSpec((2, n, rank, tile), lambda i: (0, 0, 0, i))],
+        in_specs=[
+            smem,
+            smem,
+            pl.BlockSpec((2, n, rank, tile), lambda i: (0, 0, 0, i)),
+            pl.BlockSpec((2, rank, tile), lambda i: (0, 0, i)),
+            pl.BlockSpec((2, rank, columns), lambda i: (0, 0, 0)),
+        ],
         out_specs=(
+            pl.BlockSpec((tile, columns), lambda i: (i, 0)),
+            pl.BlockSpec((tile, columns), lambda i: (i, 0)),
             pl.BlockSpec((own, rank, tile), lambda i: (0, 0, i)),
             pl.BlockSpec((own, rank, tile), lambda i: (0, 0, i)),
         ),
         compiler_params=pltpu.CompilerParams(vmem_limit_bytes=60 * 1024 * 1024),
         name="collect",
-    )(slots, base, terms)
-    return delta_t, grad_input_t, grad_down, grad_up
+    )(slots, base, terms, mine, ranks)
 
 
 def solution(mesh):

time: 72.1 us -> 69.8 us (0.968)
  local copies, waits for them, and re-layouts: 1.95 us -> 0 us
    unnamed x6 -> x0, local copies, waits for them, and re-layouts: 1.95 us -> none
where the time goes in v3:
time: 69.8 us; the launch traced here: 69.7 us
  Pallas kernels  67.7 us (97%)
  between operations  1.94 us (3%)
    pallas_call x1, Pallas kernels, shards(): pl.pallas_call(functools.partial(exchange, n), out_shape=(jax.ShapeDtypeS...  63.3 us
    pallas_call x1, Pallas kernels, shards(): pl.pallas_call(functools.partial(collect, n), grid=(width // tile,), out_...  4.42 us

profile of v3, /device:TPU:0, one launch (start us, length us, event | category | flops | bytes accessed | tf_op | source)
XLA Modules:
  0.0 69.7 jit_solution(17178331931973528207)
XLA Ops:
  1.9 63.3 %exchange.1 = (bf16[2,16,4096]{2,1,0:T(8,128)(2,1)}, bf16[2,16,128]{2,1,0:T(8,128)(2,1)}, bf16[2,8,16,4096]{3,2,1,0:T(8,128)(2,1)}, s32[8,1,128]{2,1,0:T(1,128)}) custom-call(s32[1]{0:T(128)S(6)} %copy.11.tenant_ref, s32[1]{0:T(128)S(6)} %copy.12.rows_ref, s32[64]{0:T(128)} %owner_ref.1, bf16[4096,128]{1,0:T(8,128)(2,1)} %in_hbm.1, ...), custom_call_target="tpu_custom_call" | custom-call | tf_op jit(solution)/shard_map/exchange/pallas_call | solution.py:312
  65.2 4.4 %collect.1 = (bf16[4096,128]{1,0:T(8,128)(2,1)}, bf16[4096,128]{1,0:T(8,128)(2,1)}, f32[8,16,4096]{2,1,0:T(8,128)}, f32[8,16,4096]{2,1,0:T(8,128)}) custom-call(s32[8,1,128]{2,1,0:T(1,128)} %get-tuple-element.8.slots_ref, s32[1]{0:T(128)} %bitcast.base_ref, bf16[2,8,16,4096]{3,2,1,0:T(8,128)(2,1)} %get-tuple-element.9.terms_ref, ...), custom_call_target="tpu_custom_call" | custom-call | tf_op jit(solution)/shard_map/collect/pallas_call | solution.py:355

commit v4 on v3

--- a/solution.py
+++ b/solution.py
@@ -11,6 +11,7 @@
 F32 = jnp.float32
 LANES = 4
 WAYS = tuple(1 if w < LANES // 2 else -1 for w in range(LANES))
+ORDER = tuple(w // 2 + (w % 2) * (LANES // 2) for w in range(LANES))
 
 
 def place_of(dev, n):
@@ -109,7 +110,7 @@
         blocks = [dev_of(p - way * (1 + step), n) for way in (1, -1)]
         chosen = [masks(block) for block in blocks]
         for a in range(2):
-            for w in range(LANES):
+            for w in ORDER:
                 ready[a, w] = share(a, w, chosen[(1 - WAYS[w]) // 2])
 
     def target(w):
@@ -125,7 +126,7 @@
 
     for a in range(2):
         chosen = [masks(dev_of(p - way, n)) for way in (1, -1)]
-        for w in range(LANES):
+        for w in ORDER:
             first[a, w] = share(a, w, chosen[(1 - WAYS[w]) // 2])
             rs_copy(a, w, 0, first.at[a, w]).start()
     prepare(1)
@@ -133,7 +134,7 @@
     def rs_step(step, _):
         here = lax.rem(step - 1, depth)
         for a in range(2):
-            for w in range(LANES):
+            for w in ORDER:
                 rs_copy(a, w, step - 1, first.at[a, w]).wait_recv()
                 moving[a, w, here] = moving[a, w, here] + ready[a, w]
                 if depth < n - 1:
@@ -169,7 +170,7 @@
         )
 
     for a in range(2):
-        for w in range(LANES):
+        for w in ORDER:
             rs_copy(a, w, n - 2, first.at[a, w]).wait_recv()
             got = moving[a, w, (n - 2) % depth] + ready[a, w]
             mine[a, :, cut(w)] = got
@@ -209,7 +210,7 @@
     for a in range(2):
         part_copy(a).wait_recv()
         ranks[a] = ((part_mine[a] + part_other[a]) * keep).astype(BF)
-        for w in range(LANES):
+        for w in ORDER:
             terms[a, d, :, cut(w)] = lax.dot_general(
                 ranks[a], tokens[1 - a, cut(w), :],
                 (((1,), (1,)), ((), ())), preferred_element_type=F32,
@@ -228,7 +229,7 @@
 
     def ag_step(step):
         for a in range(2):
-            for w in range(LANES):
+            for w in ORDER:
                 ag_arrive(a, w, step - 1).wait_recv()
                 ag_copy(a, w, step).start()
             for r in range(2):
@@ -236,7 +237,7 @@
 
     lax.fori_loop(1, n - 1, lambda k, c: (ag_step(k), c)[1], 0)
     for a in range(2):
-        for w in range(LANES):
+        for w in ORDER:
             ag_arrive(a, w, n - 2).wait_recv()
         for r in range(2):
             keep_copy(a, r, n - 1).start()
@@ -249,7 +250,7 @@
 
     def rs_end(step, c):
         for a in range(2):
-            for w in range(LANES):
+            for w in ORDER:
                 rs_copy(a, w, step, first.at[a, w]).wait_send()
         return c
 
@@ -257,7 +258,7 @@
 
     def ag_end(step, c):
         for a in range(2):
-            for w in range(LANES):
+            for w in ORDER:
                 ag_copy(a, w, step).wait_send()
         return c
 
@@ -293,7 +294,7 @@
 
         return c
 
-    lax.fori_loop(0, n, add, 0)
+    lax.fori_loop(0, n, add, 0, unroll=min(n, 8))
     for a, out in enumerate((delta_ref, gin_ref)):
         out[...] = lax.dot_general(
             mine_ref[1 - a], ranks_ref[a] + ranks_ref[a],

time: 69.8 us -> 68 us (0.974)
  Pallas kernels: 67.7 us -> 65.9 us
    pallas_call x1, Pallas kernels: 63.3 us -> 61.6 us  [shards(): pl.pallas_call(functools.partial(exchange, n), out_shape=(jax.ShapeDtypeS...]
where the time goes in v4:
time: 68 us; the launch traced here: 67.8 us
  Pallas kernels  65.9 us (97%)
  between operations  1.94 us (3%)
    pallas_call x1, Pallas kernels, shards(): pl.pallas_call(functools.partial(exchange, n), out_shape=(jax.ShapeDtypeS...  61.6 us
    pallas_call x1, Pallas kernels, shards(): pl.pallas_call(functools.partial(collect, n), grid=(width // tile,), out_...  4.27 us

profile of v4, /device:TPU:0, one launch (start us, length us, event | category | flops | bytes accessed | tf_op | source)
XLA Modules:
  0.0 67.8 jit_solution(13339051584670213588)
XLA Ops:
  1.9 61.6 %exchange.1 = (bf16[2,16,4096]{2,1,0:T(8,128)(2,1)}, bf16[2,16,128]{2,1,0:T(8,128)(2,1)}, bf16[2,8,16,4096]{3,2,1,0:T(8,128)(2,1)}, s32[8,1,128]{2,1,0:T(1,128)}) custom-call(s32[1]{0:T(128)S(6)} %copy.11.tenant_ref, s32[1]{0:T(128)S(6)} %copy.12.rows_ref, s32[64]{0:T(128)} %owner_ref.1, bf16[4096,128]{1,0:T(8,128)(2,1)} %in_hbm.1, ...), custom_call_target="tpu_custom_call" | custom-call | tf_op jit(solution)/shard_map/exchange/pallas_call | solution.py:313
  63.6 4.3 %collect.1 = (bf16[4096,128]{1,0:T(8,128)(2,1)}, bf16[4096,128]{1,0:T(8,128)(2,1)}, f32[8,16,4096]{2,1,0:T(8,128)}, f32[8,16,4096]{2,1,0:T(8,128)}) custom-call(s32[8,1,128]{2,1,0:T(1,128)} %get-tuple-element.8.slots_ref, s32[1]{0:T(128)} %bitcast.base_ref, bf16[2,8,16,4096]{3,2,1,0:T(8,128)(2,1)} %get-tuple-element.9.terms_ref, ...), custom_call_target="tpu_custom_call" | custom-call | tf_op jit(solution)/shard_map/collect/pallas_call | solution.py:356
